TPU v7x, 128 devices: a whole 4x4x4 slice. The times are simulated.
128 devices in a mesh: owner: 16 (over z, x), worker: 8 (over y, core).
Axes of the slice: x: 4, y: 4, z: 4, core: 2. Of those that a mesh axis runs over, the one named last changes fastest.
Arguments:
- embeddings: bfloat16 [262144, 4096], P(('owner', 'worker')), may hold values from -6 to 6
- row_cluster: int32 [262144], P(('owner', 'worker')), may hold values from 0 to 63
- block_owner: int32 [2048], P(('owner', 'worker')), may hold values from 0 to 15, as said below
- routing: int32 [16, 8, 16], replicated, may hold values from 0 to 7, as said below
Outputs:
- row_best: float32 [262144], P(('owner', 'worker'))
Inputs may be any that keep to these rules, and one draw needn't show every extreme that they name: `block_owner`: the 16 blocks of one device go to 16 different owner indices, each owner index once. routing[p, w, o] is the worker index to which device (p, w) passes on the block that device (o, w) sends to owner p. For fixed p and o the 8 values over w all differ; for fixed p and w (over o), and for fixed o and w (over p), every worker index is named exactly 2 times.
All inputs are finite; a program needn't handle non-finite values.
Results may differ from a plain program's by a relative error of at most 0.0003.
Values may be sent and summed in bfloat16 or wider, within the bound.
A program may use at most 128 MiB of HBM per device.

v0:
```python
import jax
import jax.numpy as jnp
from jax import lax
from jax.sharding import PartitionSpec as P


def tile_scores(
    queries, keys_block, query_labels, key_labels, query_scales, key_scales, query_start, key_start
):
    feature_width = queries.shape[1]
    products = jnp.dot(queries, keys_block.T, preferred_element_type=jnp.float32)
    cosine = products * query_scales[:, None] * key_scales[None, :] / feature_width
    query_index = query_start + jnp.arange(queries.shape[0], dtype=jnp.int32)
    key_index = key_start + jnp.arange(keys_block.shape[0], dtype=jnp.int32)
    allowed = (query_labels[:, None] == key_labels[None, :]) & (
        query_index[:, None] != key_index[None, :]
    )
    return jnp.where(allowed, cosine, -1.0)


def group_maxima(members, member_labels):
    total_rows = members.shape[0]
    member_scales = lax.rsqrt(jnp.mean(jnp.square(members.astype(jnp.float32)), axis=1) + 1e-06)
    piece_rows = min(512, total_rows)
    piece_count = total_rows // piece_rows

    def take_piece(values, index):
        return values[index * piece_rows : (index + 1) * piece_rows]

    running = [jnp.full((piece_rows,), -1.0, jnp.float32) for index in range(piece_count)]
    for first in range(piece_count):
        for second in range(first, piece_count):
            scores = tile_scores(
                take_piece(members, first),
                take_piece(members, second),
                take_piece(member_labels, first),
                take_piece(member_labels, second),
                take_piece(member_scales, first),
                take_piece(member_scales, second),
                first * piece_rows,
                second * piece_rows,
            )
            running[first] = jnp.maximum(running[first], jnp.max(scores, axis=1))
            if second != first:
                running[second] = jnp.maximum(running[second], jnp.max(scores, axis=0))
    return jnp.concatenate(running)


def shards(embeddings, row_cluster, block_owner, routing):
    owner_count = lax.axis_size("owner")
    worker_count = lax.axis_size("worker")
    slot_count = owner_count // worker_count
    block_count = block_owner.shape[0]
    block_rows = embeddings.shape[0] // block_count
    feature_width = embeddings.shape[1]
    blocks = embeddings.reshape(block_count, block_rows, feature_width)
    labels = row_cluster.reshape(block_count, block_rows)
    my_owner = lax.axis_index("owner")
    my_worker = lax.axis_index("worker")
    owner_iota = jnp.arange(owner_count, dtype=jnp.int32)
    send_order = jnp.argmax(block_owner[None, :] == owner_iota[:, None], axis=1)
    outgoing = blocks[send_order]
    outgoing_labels = labels[send_order]
    arrived, arrived_labels = (
        lax.all_to_all(outgoing, "owner", split_axis=0, concat_axis=0, tiled=True),
        lax.all_to_all(outgoing_labels, "owner", split_axis=0, concat_axis=0, tiled=True),
    )
    route_row = routing[my_owner, my_worker]
    pass_order = jnp.argsort(route_row, stable=True)
    forward = arrived[pass_order].reshape(worker_count, slot_count, block_rows, feature_width)
    forward_labels = arrived_labels[pass_order].reshape(worker_count, slot_count, block_rows)
    gathered, gathered_labels = (
        lax.all_to_all(forward, "worker", split_axis=0, concat_axis=0, tiled=True),
        lax.all_to_all(forward_labels, "worker", split_axis=0, concat_axis=0, tiled=True),
    )
    members = gathered.reshape(-1, feature_width)
    member_labels = gathered_labels.reshape(-1)
    maxima = group_maxima(members, member_labels).reshape(worker_count, slot_count, block_rows)
    returned = lax.all_to_all(maxima, "worker", split_axis=0, concat_axis=0, tiled=True).reshape(
        owner_count, block_rows
    )
    relayed = returned[jnp.argsort(pass_order)]
    arrived_home = lax.all_to_all(relayed, "owner", split_axis=0, concat_axis=0, tiled=True)
    results = arrived_home[block_owner]
    return results.reshape(-1)


def solution(mesh):
    placed = (P(("owner", "worker"), None), P(("owner", "worker")), P(("owner", "worker")), P())
    return jax.shard_map(
        shards, mesh=mesh, in_specs=placed, out_specs=P(("owner", "worker")), check_vma=False
    )
```

profile of v0, /device:TPU:1, one launch (start us, length us, event | category | flops | bytes accessed | tf_op | source)
XLA Modules:
  0.0 549.5 jit_solution(9288488784490723728)
XLA Ops:
  0.0 0.0 copy-start
  0.0 1.3 iota_reduce_fusion
  1.3 1.8 gather_fusion
  3.2 8.4 %all-to-all-start = ((s32[16,1,128]{2,1,0:T(1,128)}), s32[16,1,128]{2,1,0:T(1,128)S(1)}, u32[]{:S(2)}, u32[]{:S(2)}) async-start(s32[16,1,128]{2,1,0:T(1,128)} %bitcast.2), calls=%async_computation | async-start | bytes 16384 | tf_op jit(solution)/shard_map/all_to_all | solution.py:66
  11.6 13.0 %gather_fusion.2 = bf16[16,128,4096]{2,1,0:T(8,128)(2,1)} fusion(bf16[16,128,4096]{2,1,0:T(8,128)(2,1)} %bitcast.53, s32[1024]{0:T(1024)S(1)} %pad_clamp_fusion.3), kind=kCustom, calls=%fused_computation.2 | custom fusion | bytes 33554496 | tf_op jit(solution)/shard_map/gather | solution.py:62
  24.6 0.0 all-to-all-done
  24.6 6.7 %all-to-all-start.2 = ((bf16[16,128,4096]{2,1,0:T(8,128)(2,1)}), bf16[16,128,4096]{2,1,0:T(8,128)(2,1)}, u32[]{:S(2)}, u32[]{:S(2)}) async-start(bf16[16,128,4096]{2,1,0:T(8,128)(2,1)} %gather_fusion.2), calls=%async_computation.2 | async-start | bytes 33554432 | tf_op jit(solution)/shard_map/all_to_all | solution.py:65
  31.4 0.0 copy-done
  31.4 1.2 sort.34
  32.7 1.2 gather_fusion.1
  33.8 243.2 %all-to-all-done.2 = bf16[16,128,4096]{2,1,0:T(8,128)(2,1)} async-done(((bf16[16,128,4096]{2,1,0:T(8,128)(2,1)}), bf16[16,128,4096]{2,1,0:T(8,128)(2,1)}, u32[]{:S(2)}, u32[]{:S(2)}) %all-to-all-start.2) | async-done | bytes 16777248 | tf_op jit(solution)/shard_map/all_to_all | solution.py:65
  277.0 6.9 %all-to-all-start.1 = ((s32[8,2,128]{2,1,0:T(2,128)}), s32[8,2,128]{2,1,0:T(2,128)S(1)}, u32[]{:S(2)}, u32[]{:S(2)}) async-start(s32[8,2,128]{2,1,0:T(2,128)} %bitcast.5), calls=%async_computation.1 | async-start | bytes 16384 | tf_op jit(solution)/shard_map/all_to_all | solution.py:74
  283.9 13.0 %gather_fusion.3 = bf16[16,128,4096]{2,1,0:T(8,128)(2,1)} fusion(bf16[16,128,4096]{2,1,0:T(8,128)(2,1)} %all-to-all-done.2, s32[1024]{0:T(1024)S(1)} %pad_clamp_fusion.2), kind=kCustom, calls=%fused_computation.3 | custom fusion | bytes 33554496 | tf_op jit(solution)/shard_map/gather | solution.py:70
  296.9 0.0 all-to-all-done.1
  296.9 0.0 copy-start.2
  296.9 5.8 %all-to-all-start.3 = ((bf16[8,2,128,4096]{3,2,1,0:T(8,128)(2,1)}), bf16[8,2,128,4096]{3,2,1,0:T(8,128)(2,1)}, u32[]{:S(2)}, u32[]{:S(2)}) async-start(bf16[8,2,128,4096]{3,2,1,0:T(8,128)(2,1)} %bitcast.52), calls=%async_computation.3 | async-start | bytes 33554432 | tf_op jit(solution)/shard_map/all_to_all | solution.py:73
  302.7 1.2 sort.35
  304.0 0.0 copy-done.2
  304.0 182.4 %all-to-all-done.3 = bf16[8,2,128,4096]{3,2,1,0:T(8,128)(2,1)} async-done(((bf16[8,2,128,4096]{3,2,1,0:T(8,128)(2,1)}), bf16[8,2,128,4096]{3,2,1,0:T(8,128)(2,1)}, u32[]{:S(2)}, u32[]{:S(2)}) %all-to-all-start.3) | async-done | bytes 16777248 | tf_op jit(solution)/shard_map/all_to_all | solution.py:73
  486.4 7.2 %multiply_reduce_fusion = f32[8,2,128]{2,1,0:T(2,128)S(1)} fusion(bf16[8,2,128,4096]{3,2,1,0:T(8,128)(2,1)} %all-to-all-done.3), kind=kLoop, calls=%fused_computation.6 | loop fusion | flops 25163776 | bytes 16785408 | tf_op jit(solution)/shard_map/reduce_sum | solution.py:23
  493.6 6.6 %fusion.44 = (bf16[2,2,128,4096]{3,2,1,0:T(8,128)(2,1)S(1)}, bf16[2,2,128,4096]{3,2,1,0:T(8,128)(2,1)S(1)}, bf16[2,2,128,4096]{3,2,1,0:T(8,128)(2,1)S(1)}, bf16[2,2,128,4096]{3,2,1,0:T(8,128)(2,1)S(1)}) fusion(bf16[8,2,128,4096]{3,2,1,0:T(8,128)(2,1)} %all-to-all-done.3), kind=kLoop, calls=%fused_computation.85 | loop fusion | bytes 33554432 | tf_op jit(solution)/shard_map/slice | solution.py:28
  500.3 2.6 fusion.38
  502.9 2.6 fusion.39
  505.6 2.6 fusion.41
  508.2 2.6 fusion.40
  510.8 2.6 fusion.42
  513.4 2.8 fusion.31
  516.2 2.5 fusion.30
  518.7 2.6 fusion.43
  521.3 2.5 fusion.32
  523.8 0.0 copy-start.1
  523.9 2.5 fusion.33
  526.4 0.6 pad_maximum_fusion
  527.0 4.1 all-to-all-start.4
  531.2 4.6 all-to-all-done.4
  535.8 1.2 gather_fusion.4
  536.9 5.1 all-to-all-start.5
  542.0 6.3 %all-to-all-done.5 = f32[16,1,128]{2,1,0:T(1,128)S(1)} async-done(((f32[16,1,128]{2,1,0:T(1,128)}), f32[16,1,128]{2,1,0:T(1,128)S(1)}, u32[]{:S(2)}, u32[]{:S(2)}) %all-to-all-start.5) | async-done | bytes 8224 | tf_op jit(solution)/shard_map/all_to_all | solution.py:83
  548.3 1.2 gather_fusion.5
  549.5 0.0 copy-done.1
  (19 shorter events, 0.1 us)
Async XLA Ops:
  0.0 31.4 %copy-start = (s32[16,8,16]{2,1,0:T(8,128)S(1)}, s32[16,8,16]{2,1,0:T(8,128)}, u32[]{:S(2)}) copy-start(s32[16,8,16]{2,1,0:T(8,128)} %param.7) | copy-start | bytes 24580
  3.2 21.5 %all-to-all-start = ((s32[16,1,128]{2,1,0:T(1,128)}), s32[16,1,128]{2,1,0:T(1,128)S(1)}, u32[]{:S(2)}, u32[]{:S(2)}) async-start(s32[16,1,128]{2,1,0:T(1,128)} %bitcast.2), calls=%async_computation | async-start | bytes 16384 | tf_op jit(solution)/shard_map/all_to_all | solution.py:66
  24.6 252.4 %all-to-all-start.2 = ((bf16[16,128,4096]{2,1,0:T(8,128)(2,1)}), bf16[16,128,4096]{2,1,0:T(8,128)(2,1)}, u32[]{:S(2)}, u32[]{:S(2)}) async-start(bf16[16,128,4096]{2,1,0:T(8,128)(2,1)} %gather_fusion.2), calls=%async_computation.2 | async-start | bytes 33554432 | tf_op jit(solution)/shard_map/all_to_all | solution.py:65
  277.0 19.9 %all-to-all-start.1 = ((s32[8,2,128]{2,1,0:T(2,128)}), s32[8,2,128]{2,1,0:T(2,128)S(1)}, u32[]{:S(2)}, u32[]{:S(2)}) async-start(s32[8,2,128]{2,1,0:T(2,128)} %bitcast.5), calls=%async_computation.1 | async-start | bytes 16384 | tf_op jit(solution)/shard_map/all_to_all | solution.py:74
  296.9 7.1 %copy-start.2 = (s32[16]{0:T(128)S(1)}, s32[16]{0:T(128)}, u32[]{:S(2)}) copy-start(s32[16]{0:T(128)} %param.6) | copy-start | bytes 196
  296.9 189.5 %all-to-all-start.3 = ((bf16[8,2,128,4096]{3,2,1,0:T(8,128)(2,1)}), bf16[8,2,128,4096]{3,2,1,0:T(8,128)(2,1)}, u32[]{:S(2)}, u32[]{:S(2)}) async-start(bf16[8,2,128,4096]{3,2,1,0:T(8,128)(2,1)} %bitcast.52), calls=%async_computation.3 | async-start | bytes 33554432 | tf_op jit(solution)/shard_map/all_to_all | solution.py:73
  523.8 25.6 %copy-start.1 = (s32[16,8,16]{2,1,0:T(8,128)S(1)}, s32[16,8,16]{2,1,0:T(8,128)}, u32[]{:S(2)}) copy-start(s32[16,8,16]{2,1,0:T(8,128)} %param.7) | copy-start | bytes 24580
  527.0 8.8 %all-to-all-start.4 = ((f32[8,2,128]{2,1,0:T(2,128)}), f32[8,2,128]{2,1,0:T(2,128)S(1)}, u32[]{:S(2)}, u32[]{:S(2)}) async-start(f32[8,2,128]{2,1,0:T(2,128)} %pad_maximum_fusion), calls=%async_computation.4 | async-start | bytes 16384 | tf_op jit(solution)/shard_map/all_to_all | solution.py:79
  536.9 11.4 %all-to-all-start.5 = ((f32[16,1,128]{2,1,0:T(1,128)}), f32[16,1,128]{2,1,0:T(1,128)S(1)}, u32[]{:S(2)}, u32[]{:S(2)}) async-start(f32[16,1,128]{2,1,0:T(1,128)} %bitcast.26), calls=%async_computation.5 | async-start | bytes 16384 | tf_op jit(solution)/shard_map/all_to_all | solution.py:83
where the time goes:
time: 551 us; the launch traced here: 549 us
  waiting for transfers between devices  437 us (79%)
  local copies, waits for them, and re-layouts  38 us (7%)
  starting transfers between devices  37 us (7%)
  matrix products  26 us (5%)
  other arithmetic  11.7 us (2%)
    all_to_all x1, waiting for transfers between devices, shards(): lax.all_to_all(outgoing, 'owner', split_axis=0, concat_axis=0, tiled=True)  243 us
    all_to_all x1, waiting for transfers between devices, shards(): lax.all_to_all(forward, 'worker', split_axis=0, concat_axis=0, tiled=True)  182 us
    dot_general x10, matrix products, tile_scores(): jnp.dot(queries, keys_block.T, preferred_element_type=jnp.float32)  26 us
    gather x1, local copies, waits for them, and re-layouts, shards(): outgoing = blocks[send_order]  13 us
    gather x1, local copies, waits for them, and re-layouts, shards(): arrived[pass_order]  13 us
  transfers between devices with their start and end apart: 6, of which 4 were waited for; matrix products, arithmetic and copies ran while one was open for 5% of the time, Pallas kernels for 0%

commit v1 on v0

v1 whole, which is shorter than its diff:
```python
import jax
import jax.numpy as jnp
from jax import lax
from jax.experimental import pallas as pl
from jax.experimental.pallas import tpu as pltpu
from jax.sharding import PartitionSpec as P

MESH = pl.DeviceIdType.MESH
CHUNKS = 8
ROWS = 16
WIDTH = 4096
TILE = 256
NEG = -3.0e38
KIND = "AABBCCDD"
Y_STEPS = ((1, 0), (3, 1), (2, 0), (1, 1), (3, 0), (2, 1), (0, 1))
O_STEPS = tuple((a, b) for a in range(4) for b in range(4) if (a, b) != (0, 0))
ARRIVALS = (0, 1, 2, 4, 6, 3, 5, 7)


def kernel(tab, emb, lab, out, r1, *scratch):
    sends = scratch[0:8]
    mids = scratch[8:16]
    (
        members, stage0, stage1, lab_a, lab_b, lab_c, lab_d, lab_e, label_rows, scale_rows, best_rows, lane_best,
        result, gathered, relayed, home, send_sem, recv_sem, local_sem, stage_sem,
        res_send, res_recv, home_send, home_recv,
    ) = scratch[16:]
    owner = lax.axis_index("owner")
    worker = lax.axis_index("worker")
    mz, mx = owner // 4, owner % 4
    my, mc = worker // 2, worker % 2

    def turn(value, step, size):
        return lax.rem(value + step, size)

    def owner_of(dz, dx):
        return turn(mz, dz, 4) * 4 + turn(mx, dx, 4)

    def worker_of(dy, dc):
        return turn(my, dy, 4) * 2 + turn(mc, dc, 2)

    barrier = pltpu.get_barrier_semaphore()
    for dz, dx in O_STEPS:
        pl.semaphore_signal(barrier, inc=1, device_id=(owner_of(dz, dx), worker), device_id_type=MESH)
    for dy, dc in Y_STEPS:
        pl.semaphore_signal(barrier, inc=1, device_id=(owner, worker_of(dy, dc)), device_id_type=MESH)

    def remote(src, dst, send, recv, to):
        return pltpu.make_async_remote_copy(
            src_ref=src, dst_ref=dst, send_sem=send, recv_sem=recv, device_id=to, device_id_type=MESH
        )

    def hop(axis, src, dst, n, stage):
        copies = []
        if axis == "z":
            for i, d in enumerate((1, 3, 2)):
                to = turn(mz, d, 4)
                copies.append(
                    remote(src.at[to], dst.at[mz], send_sem.at[n, stage, i], recv_sem.at[n, stage, i], (to * 4 + mx, worker))
                )
            here = (src.at[mz], dst.at[mz])
        elif axis == "x":
            for i, d in enumerate((1, 3, 2)):
                to = turn(mx, d, 4)
                copies.append(
                    remote(src.at[:, to], dst.at[:, mx], send_sem.at[n, stage, i], recv_sem.at[n, stage, i], (mz * 4 + to, worker))
                )
            here = (src.at[:, mx], dst.at[:, mx])
        else:
            for i, (dy, dc) in enumerate(Y_STEPS):
                to = worker_of(dy, dc)
                copies.append(
                    remote(
                        src.at[to // 2, pl.ds(2 * lax.rem(to, 2), 2)], dst.at[my, pl.ds(2 * mc, 2)],
                        send_sem.at[n, stage, i], recv_sem.at[n, stage, i], (owner, to),
                    )
                )
            here = (src.at[my, pl.ds(2 * mc, 2)], dst.at[my, pl.ds(2 * mc, 2)])
        copies.append(pltpu.make_async_copy(here[0], here[1], local_sem.at[n, stage]))
        return copies

    flying = {}

    def start(n, stage, axis, src, dst):
        flying[n, stage] = hop(axis, src, dst, n, stage)
        for copy in flying[n, stage]:
            copy.start()

    def wait(n, stage):
        for copy in flying[n, stage][:-1]:
            copy.wait_recv()
            copy.wait_send()
        flying[n, stage][-1].wait()

    def permute(row, src, dst, flat=False):
        def body(slot, carry):
            index = tab[row, slot]
            if flat:
                dst[slot >> 2, slot & 3] = src[index]
            else:
                dst[slot >> 2, slot & 3] = src[index >> 2, index & 3]
            return carry

        lax.fori_loop(0, 16, body, 0)

    def route(n):
        if n == CHUNKS:
            return (("z", lab_a, lab_b), ("x", lab_b, lab_c), ("y", lab_d, lab_e))
        s, r, m, f = sends[n], r1.at[n], mids[n], members.at[ARRIVALS.index(n)]
        return {
            "A": (("z", s, r), ("x", r, m), ("y", s, f)),
            "B": (("x", s, r), ("z", r, m), ("y", s, f)),
            "C": (("y", s, m), ("z", s, r), ("x", r, f)),
            "D": (("y", s, m), ("x", s, r), ("z", r, f)),
        }[KIND[n]]

    def go(n, stage):
        start(n, stage, *route(n)[stage])

    def middle(n):
        if n == CHUNKS:
            permute(2, lab_c, lab_d)
        else:
            permute(2 if KIND[n] in "AB" else 3, mids[n], sends[n])

    stages = (stage0, stage1)

    def fetch(n, at):
        return pltpu.make_async_copy(emb.at[:, pl.ds(ROWS * n, ROWS), :], stages[at], stage_sem.at[at])

    first = (0, 2, 4, 1, 3, 5, 6, 7)
    fetch(first[0], 0).start()
    fetch(first[1], 1).start()
    permute(0, lab, lab_a, flat=True)
    for i, n in enumerate(first):
        fetch(n, i % 2).wait()
        permute(0 if KIND[n] in "AB" else 1, stages[i % 2], sends[n], flat=True)
        if i + 2 < len(first):
            fetch(first[i + 2], i % 2).start()
        if i == 0:
            pl.semaphore_wait(barrier, len(O_STEPS) + len(Y_STEPS))
        if KIND[n] != "D":
            go(n, 0)
        if i == 2:
            go(CHUNKS, 0)

    lane = lax.broadcasted_iota(jnp.int32, (1, TILE), 1)
    eye = lax.broadcasted_iota(jnp.int32, (TILE, TILE), 0) == lax.broadcasted_iota(jnp.int32, (TILE, TILE), 1)

    def as_column(row):
        column = jnp.transpose(jnp.broadcast_to(row, (128, TILE)))
        return jnp.concatenate([column, column], axis=1)

    def product(a, b):
        return lax.dot_general(a, b, (((1,), (1,)), ((), ())), preferred_element_type=jnp.float32)

    def chunk_of(i):
        return members[i].reshape(TILE, WIDTH)

    def gram(i):
        n = ARRIVALS[i]
        row = jnp.zeros((1, TILE), jnp.float32)
        for slot in range(16):
            if KIND[n] in "AB":
                tile = lab_e[slot // 4, slot % 4]
            else:
                index = tab[4, slot]
                tile = lab_e[index >> 2, index & 3]
            row = jnp.where(lane // 16 == slot, tile[n : n + 1, :], row)
        label_rows[i] = jnp.broadcast_to(row, (8, TILE))
        labels = as_column(row)
        own = product(chunk_of(i), chunk_of(i))
        scale = lax.rsqrt(jnp.sum(jnp.where(eye, own, 0.0), axis=0, keepdims=True) / WIDTH + 1e-6)
        scale_rows[i] = jnp.broadcast_to(scale, (8, TILE))
        scales = as_column(scale)
        scored = jnp.where((labels == row) & jnp.logical_not(eye), own * scales, NEG)
        best_rows[i] = jnp.broadcast_to(jnp.max(scored, axis=0, keepdims=True), (8, TILE))
        lane_best[...] = jnp.full((TILE, 128), NEG, jnp.float32)

        def body(j, carry):
            other = product(chunk_of(i), chunk_of(j))
            match = labels == label_rows[j][0:1]
            down = jnp.max(jnp.where(match, other * scales, NEG), axis=0, keepdims=True)
            best_rows[j] = jnp.maximum(best_rows[j], jnp.broadcast_to(down, (8, TILE)))
            across = jnp.where(match, other * scale_rows[j][0:1], NEG)
            lane_best[...] = jnp.maximum(lane_best[...], jnp.maximum(across[:, :128], across[:, 128:]))
            return carry

        if i > 0:
            lax.fori_loop(0, i, body, 0)
            turned = jnp.max(jnp.transpose(lane_best[...]), axis=0, keepdims=True)
            best_rows[i] = jnp.maximum(best_rows[i], jnp.broadcast_to(turned, (8, TILE)))

    wait(0, 0); go(0, 1)
    wait(2, 0); go(2, 1)
    wait(4, 0); go(6, 0); middle(4)
    wait(8, 0); go(8, 1)
    wait(1, 0); go(1, 1)
    wait(3, 0); go(3, 1)
    wait(5, 0); go(7, 0); go(4, 1); middle(5)
    wait(0, 1); middle(0); go(0, 2)
    wait(8, 1); middle(8); go(8, 2)
    wait(2, 1); middle(2)
    wait(6, 0); middle(6); go(6, 1)
    wait(1, 1); middle(1); go(1, 2)
    go(5, 1)
    wait(3, 1); middle(3)
    wait(7, 0); middle(7); go(7, 1)
    wait(0, 2); go(2, 2)
    wait(4, 1); go(4, 2)
    wait(6, 1); go(6, 2)
    wait(8, 2); gram(0)
    wait(1, 2); go(3, 2)
    wait(5, 1); go(5, 2)
    wait(7, 1); go(7, 2)
    gram(1)
    wait(2, 2); gram(2)
    wait(4, 2); gram(3)
    wait(6, 2); gram(4)
    wait(3, 2); gram(5)
    wait(5, 2); gram(6)
    wait(7, 2); gram(7)

    for i, n in enumerate(ARRIVALS):
        result[n : n + 1, :] = jnp.maximum(best_rows[i][0:1] * scale_rows[i][0:1] / WIDTH, -1.0)
    back = [
        remote(result, gathered.at[worker], res_send.at[i], res_recv.at[i], (owner, worker_of(dy, dc)))
        for i, (dy, dc) in enumerate(Y_STEPS)
    ]
    for copy in back:
        copy.start()
    gathered[worker] = result[...]
    for copy in back:
        copy.wait()

    def relay(slot, carry):
        relayed[slot] = gathered[tab[5, slot]]
        return carry

    lax.fori_loop(0, 16, relay, 0)
    back = [
        remote(relayed.at[owner_of(dz, dx)], home.at[owner], home_send.at[i], home_recv.at[i], (owner_of(dz, dx), worker))
        for i, (dz, dx) in enumerate(O_STEPS)
    ]
    for copy in back:
        copy.start()
    home[owner] = relayed[owner]
    for copy in back:
        copy.wait()

    chunk = lax.broadcasted_iota(jnp.int32, (8, TILE), 0)
    place = lax.broadcasted_iota(jnp.int32, (8, TILE), 1) // 16
    chunk_half = lax.broadcasted_iota(jnp.int32, (8, 128), 0)
    place_half = lax.broadcasted_iota(jnp.int32, (8, 128), 1) // 16

    def unpack(block, carry):
        tile = home[tab[7, block]]
        kept = jnp.where(place == jnp.where(chunk < 4, tab[6, block], owner), tile, 0.0)
        kept = kept[:, :128] + kept[:, 128:]
        for shift in (64, 32, 16):
            kept = kept + pltpu.roll(kept, shift, 1)
        kept = jnp.where(place_half == chunk_half, kept, 0.0)
        out[pl.ds(block, 1), :] = jnp.sum(kept, axis=0, keepdims=True)
        return carry

    lax.fori_loop(0, 16, unpack, 0)


def tables(block_owner, routing):
    owner = lax.axis_index("owner")
    worker = lax.axis_index("worker")
    iota = jnp.arange(16, dtype=jnp.int32)
    before = iota[:, None] > iota[None, :]

    def rank(values):
        same = (values[:, None] == values[None, :]) & before
        return jnp.sum(same, axis=1, dtype=jnp.int32)

    def inverse(keys, payload):
        return jnp.sum(jnp.where(keys[None, :] == iota[:, None], payload[None, :], 0), axis=1, dtype=jnp.int32)

    sent = inverse(block_owner, iota)
    along_sources = routing[owner, worker, :]
    along_targets = routing[:, worker, owner]
    key_targets = 2 * along_targets + rank(along_targets)
    row1 = inverse(key_targets, sent)
    row2 = inverse(2 * along_sources + rank(along_sources), iota)

    def found(table):
        hit = table == worker
        count = jnp.cumsum(hit, axis=0, dtype=jnp.int32) - 1
        return jnp.sum(jnp.where(hit, 2 * jnp.arange(8, dtype=jnp.int32)[None, :] + count, 0), axis=1, dtype=jnp.int32)

    row3 = found(routing[:, :, owner])
    row4 = found(routing[owner].T)
    mine = routing[:, worker, :]
    earlier = (mine == along_targets[:, None]) & (iota[None, :] < owner)
    slot = 2 * worker + jnp.sum(earlier, axis=1, dtype=jnp.int32)
    row6 = jnp.sum(jnp.where(block_owner[:, None] == iota[None, :], slot[None, :], 0), axis=1, dtype=jnp.int32)
    return jnp.stack([sent, row1, row2, row3, row4, along_sources, row6, block_owner])


def shards(embeddings, row_cluster, block_owner, routing):
    labels = row_cluster.astype(jnp.float32).reshape(16, CHUNKS, ROWS)
    labels = jnp.tile(labels, (1, 1, 16))
    vmem = pl.BlockSpec(memory_space=pltpu.VMEM)
    anywhere = pl.BlockSpec(memory_space=pl.ANY)
    unit = (4, 4, ROWS, WIDTH)
    small = (4, 4, 8, TILE)
    out, _ = pl.pallas_call(
        kernel,
        out_shape=(
            jax.ShapeDtypeStruct((16, 128), jnp.float32),
            jax.ShapeDtypeStruct((CHUNKS, *unit), jnp.bfloat16),
        ),
        in_specs=[pl.BlockSpec(memory_space=pltpu.SMEM), anywhere, vmem],
        out_specs=(vmem, anywhere),
        scratch_shapes=[
            *[pltpu.VMEM(unit, jnp.bfloat16) for _ in range(8)],
            *[pltpu.VMEM(unit, jnp.bfloat16) for _ in range(8)],
            pltpu.VMEM((CHUNKS, *unit), jnp.bfloat16),
            *[pltpu.VMEM((16, ROWS, WIDTH), jnp.bfloat16) for _ in range(2)],
            *[pltpu.VMEM(small, jnp.float32) for _ in range(5)],
            *[pltpu.VMEM((CHUNKS, 8, TILE), jnp.float32) for _ in range(3)],
            pltpu.VMEM((TILE, 128), jnp.float32),
            pltpu.VMEM((8, TILE), jnp.float32),
            pltpu.VMEM((8, 8, TILE), jnp.float32),
            pltpu.VMEM((16, 8, TILE), jnp.float32),
            pltpu.VMEM((16, 8, TILE), jnp.float32),
            pltpu.SemaphoreType.DMA((CHUNKS + 1, 3, 7)),
            pltpu.SemaphoreType.DMA((CHUNKS + 1, 3, 7)),
            pltpu.SemaphoreType.DMA((CHUNKS + 1, 3)),
            pltpu.SemaphoreType.DMA((2,)),
            pltpu.SemaphoreType.DMA((7,)),
            pltpu.SemaphoreType.DMA((7,)),
            pltpu.SemaphoreType.DMA((15,)),
            pltpu.SemaphoreType.DMA((15,)),
        ],
        compiler_params=pltpu.CompilerParams(
            collective_id=0, has_side_effects=True, vmem_limit_bytes=62 * 2**20
        ),
        cost_estimate=pl.CostEstimate(flops=2 * 36 * 256 * 256 * 4096, bytes_accessed=64 * 2**20, transcendentals=2048),
    )(tables(block_owner, routing), embeddings.reshape(16, 128, WIDTH), labels)
    return out.reshape(-1)


def solution(mesh):
    placed = (P(("owner", "worker"), None), P(("owner", "worker")), P(("owner", "worker")), P())
    return jax.shard_map(
        shards, mesh=mesh, in_specs=placed, out_specs=P(("owner", "worker")), check_vma=False
    )
```

time: 551 us -> 239 us (0.43)
  waiting for transfers between devices: 437 us -> 0 us
  Pallas kernels: 0 us -> 226 us
  starting transfers between devices: 37 us -> 0 us
  local copies, waits for them, and re-layouts: 38 us -> 8.57 us
  matrix products: 26 us -> 0 us
  other arithmetic: 11.7 us -> 3.83 us
    all_to_all x6 -> x0, waiting for transfers between devices: 437 us -> none  [the longest x1 243 us: shards(): lax.all_to_all(outgoing, 'owner', split_axis=0, concat_axis=0, tiled=True)]
    pallas_call x0 -> x1, Pallas kernels: none -> 226 us  [shards(): pl.pallas_call(kernel, out_shape=(jax.ShapeDtypeStruct((16, 128), jnp.flo...]
    all_to_all x6 -> x0, starting transfers between devices: 37 us -> none  [the longest x1 8.43 us: shards(): lax.all_to_all(outgoing_labels, 'owner', split_axis=0, concat_axis=0, til...]
    gather x6 -> x0, local copies, waits for them, and re-layouts: 31.3 us -> none  [the longest x1 13 us: shards(): outgoing = blocks[send_order]]
    dot_general x10 -> x0, matrix products: 26 us -> none  [tile_scores(): jnp.dot(queries, keys_block.T, preferred_element_type=jnp.float32)]
    slice x3 -> x0, local copies, waits for them, and re-layouts: 6.66 us -> none  [take_piece(): return values[index * piece_rows:(index + 1) * piece_rows]]
    reduce_sum x1 -> x6, other arithmetic: 7.2 us -> 1.64 us  [the longest x1 0.91 us: tables(): jnp.sum(jnp.where(block_owner[:, None] == iota[None, :], slot[None, :], 0...]
  transfers between devices with their start and end apart: 6 -> 0, of which waited for: 4 -> 0; matrix products, arithmetic and copies ran while one was open for 5% -> 0% of each run, Pallas kernels for 0% -> 0%
where the time goes in v1:
time: 239 us
  Pallas kernels  226 us (95%)
  local copies, waits for them, and re-layouts  8.57 us (4%)
  other arithmetic  3.83 us (2%)
    pallas_call x1, Pallas kernels, shards(): pl.pallas_call(kernel, out_shape=(jax.ShapeDtypeStruct((16, 128), jnp.flo...  226 us

profile of v1, /device:TPU:1, one launch (start us, length us, event | category | flops | bytes accessed | tf_op | source)
XLA Modules:
  0.0 238.8 jit_solution(9076624225556700884)
XLA Ops:
  0.0 1.3 dynamic-slice_reduce_fusion
  1.3 0.7 fusion.4
  2.0 0.7 fusion.5
  2.7 0.2 convert_reduce_fusion.1
  2.9 0.7 multiply_add_fusion
  3.6 0.1 select_reduce_fusion.3
  3.7 0.7 fusion.2
  4.4 0.1 copy.16
  4.5 0.8 constant_dynamic-slice_fusion
  5.3 0.2 convert_reduce_fusion
  5.5 0.9 select_reduce_fusion
  6.4 0.1 select_reduce_fusion.4
  6.6 0.7 convert_element_type.24
  7.3 0.1 tile.10
  7.4 0.9 constant_dynamic-slice_fusion.1
  8.3 0.1 copy.17
  8.4 0.1 copy.15
  8.5 0.1 copy.14
  8.6 0.1 select_reduce_fusion.1
  8.8 1.3 stack.28.tab
  10.0 0.1 tile.11
  10.1 1.0 tile.12.lab
  11.2 226.4 %shard_map.46 = (f32[16,128]{1,0:T(8,128)}, bf16[8,4,4,16,4096]{4,3,2,1,0:T(8,128)(2,1)}) custom-call(s32[8,16]{1,0:T(8,128)} %stack.28.tab, bf16[16,128,4096]{2,1,0:T(8,128)(2,1)} %bitcast.34, f32[16,8,256]{2,1,0:T(8,128)} %tile.12.lab), custom_call_target="tpu_custom_call" | custom-call | flops 19327352832 | bytes 67108864 | tf_op jit(solution)/shard_map/pallas_call | solution.py:310
  237.5 1.3 copy.19
  (7 shorter events, 0.1 us)

commit v2 on v1

v2 whole, which is shorter than its diff:
```python
import jax
import jax.numpy as jnp
from jax import lax
from jax.experimental import pallas as pl
from jax.experimental.pallas import tpu as pltpu
from jax.sharding import PartitionSpec as P

MESH = pl.DeviceIdType.MESH
CHUNKS = 8
HALVES = 2
UNITS = CHUNKS * HALVES
ROWS = 16
WIDTH = 4096
PART = WIDTH // HALVES
TILE = 256
NEG = -3.0e38
FLYING = 2
AXES = {"A": "zxy", "B": "xzy", "C": "yzx", "D": "yxz"}
Y_STEPS = ((1, 0), (3, 1), (2, 0), (1, 1), (3, 0), (2, 1), (0, 1))
O_STEPS = tuple((a, b) for a in range(4) for b in range(4) if (a, b) != (0, 0))
LATE = 5
LABELS = UNITS
SENT, FIRST, MID_SOURCE, MID_TARGET, PLACES, KEY, HOME = range(7)


def kind(unit):
    return "ABCD"[unit // 4]


def chunk_of_unit(unit):
    return unit // 2


def half_of_unit(unit):
    return unit % 2


def plan():
    steps = []
    queue = {"z": [], "x": [], "y": []}
    flying = {"z": [], "x": [], "y": []}
    free_at = {"z": 0, "x": 0, "y": 0}

    def fill(axis, now):
        while queue[axis] and len(flying[axis]) < FLYING:
            unit, stage = queue[axis].pop(0)
            free_at[axis] = max(free_at[axis], now) + 1
            flying[axis].append((free_at[axis], unit, stage))
            steps.append(("go", unit, stage))

    for sub in range(4):
        for letter in range(3):
            queue[AXES["ABCD"[letter]][0]].append((4 * letter + sub, 0))
    for sub in range(4):
        queue["y"].append((12 + sub, 0))
    for _ in range(FLYING):
        for axis in "zxy":
            unit, stage = queue[axis].pop(0)
            free_at[axis] += 1
            flying[axis].append((free_at[axis], unit, stage))
            steps.append(("go", unit, stage))
    steps.append(("ready",))
    while any(flying.values()):
        now, axis = min((flying[axis][0][0], "zxy".index(axis)) for axis in "zxy" if flying[axis])
        axis = "zxy"[axis]
        _, unit, stage = flying[axis].pop(0)
        steps.append(("wait", unit, stage))
        fill(axis, now)
        if stage == 2:
            steps.append(("arrived", unit))
            continue
        if stage == (1 if kind(unit) in "AB" else 0):
            steps.append(("middle", unit))
        following = AXES[kind(unit)][stage + 1]
        queue[following].append((unit, stage + 1))
        fill(following, now)
    return steps


STEPS = plan()
ARRIVALS = tuple(step[1] // 2 for step in STEPS if step[0] == "arrived" and step[1] % 2 == 1)


def kernel(owners, routing, emb, lab, out, r1, *scratch):
    sends = scratch[0:UNITS]
    mids = scratch[UNITS : 2 * UNITS]
    (
        members, stage0, stage1, lab_0, lab_a, lab_b, lab_c, lab_d, lab_e, label_rows, scale_rows, best_rows, lane_best, partial,
        result, gathered, relayed, home, tab, send_sem, recv_sem, local_sem, stage_sem,
        res_send, res_recv, home_send, home_recv,
    ) = scratch[2 * UNITS :]
    owner = lax.axis_index("owner")
    worker = lax.axis_index("worker")
    mz, mx = owner // 4, owner % 4
    my, mc = worker // 2, worker % 2

    def turn(value, step, size):
        return lax.rem(value + step, size)

    def owner_of(dz, dx):
        return turn(mz, dz, 4) * 4 + turn(mx, dx, 4)

    def worker_of(dy, dc):
        return turn(my, dy, 4) * 2 + turn(mc, dc, 2)

    barrier = pltpu.get_barrier_semaphore()
    for dz, dx in O_STEPS:
        pl.semaphore_signal(barrier, inc=1, device_id=(owner_of(dz, dx), worker), device_id_type=MESH)
    for dy, dc in Y_STEPS:
        pl.semaphore_signal(barrier, inc=1, device_id=(owner, worker_of(dy, dc)), device_id_type=MESH)

    def remote(src, dst, send, recv, to):
        return pltpu.make_async_remote_copy(
            src_ref=src, dst_ref=dst, send_sem=send, recv_sem=recv, device_id=to, device_id_type=MESH
        )

    def hop(axis, src, dst, n, stage):
        copies = []
        if axis == "z":
            for i, d in enumerate((1, 3, 2)):
                to = turn(mz, d, 4)
                copies.append(
                    remote(src.at[to], dst.at[mz], send_sem.at[n, stage, i], recv_sem.at[n, stage, i], (to * 4 + mx, worker))
                )
            here = (src.at[mz], dst.at[mz])
        elif axis == "x":
            for i, d in enumerate((1, 3, 2)):
                to = turn(mx, d, 4)
                copies.append(
                    remote(src.at[:, to], dst.at[:, mx], send_sem.at[n, stage, i], recv_sem.at[n, stage, i], (mz * 4 + to, worker))
                )
            here = (src.at[:, mx], dst.at[:, mx])
        else:
            for i, (dy, dc) in enumerate(Y_STEPS):
                to = worker_of(dy, dc)
                copies.append(
                    remote(
                        src.at[to // 2, pl.ds(2 * lax.rem(to, 2), 2)], dst.at[my, pl.ds(2 * mc, 2)],
                        send_sem.at[n, stage, i], recv_sem.at[n, stage, i], (owner, to),
                    )
                )
            here = (src.at[my, pl.ds(2 * mc, 2)], dst.at[my, pl.ds(2 * mc, 2)])
        copies.append(pltpu.make_async_copy(here[0], here[1], local_sem.at[n, stage]))
        return copies

    flying = {}

    def wait(n, stage):
        for copy in flying[n, stage][:-1]:
            copy.wait_recv()
            copy.wait_send()
        flying[n, stage][-1].wait()

    def permute(row, src, dst, flat=False):
        def body(slot, carry):
            index = tab[row, slot]
            if flat:
                dst[slot >> 2, slot & 3] = src[index]
            else:
                dst[slot >> 2, slot & 3] = src[index >> 2, index & 3]
            return carry

        lax.fori_loop(0, 16, body, 0)

    def route(n):
        if n == LABELS:
            return "zxy", ((lab_a, lab_b), (lab_b, lab_c), (lab_d, lab_e))
        s, r, m = sends[n], r1.at[n], mids[n]
        f = members.at[half_of_unit(n), ARRIVALS.index(chunk_of_unit(n))]
        return AXES[kind(n)], ((s, r), (r, m), (s, f)) if kind(n) in "AB" else ((s, m), (s, r), (r, f))

    def go(n, stage):
        axes, ends = route(n)
        flying[n, stage] = hop(axes[stage], *ends[stage], n, stage)
        for copy in flying[n, stage]:
            copy.start()

    def middle(n):
        if n == LABELS:
            permute(MID_SOURCE, lab_c, lab_d)
        else:
            permute(MID_SOURCE if kind(n) in "AB" else MID_TARGET, mids[n], sends[n])

    def invert(row, keys, payload):
        def body(slot, carry):
            found = jnp.int32(0)
            for i in range(16):
                found += jnp.where(keys(i) == slot, payload(i), 0)
            tab[row, slot] = found & 15
            return carry

        lax.fori_loop(0, 16, body, 0)

    def ranked(row, values):
        def body(slot, carry):
            value = values(slot)
            count = jnp.int32(0)
            for i in range(16):
                count += jnp.where((values(i) == value) & (i < slot), 1, 0)
            tab[row, slot] = 2 * value + count
            return carry

        lax.fori_loop(0, 16, body, 0)

    def find(row, values):
        def body(slot, counts):
            found = jnp.int32(0)
            after = []
            for w in range(8):
                hit = values(slot, w) == worker
                found += jnp.where(hit, 2 * w + counts[w], 0)
                after.append(counts[w] + jnp.where(hit, 1, 0))
            tab[row, slot] = found & 15
            return tuple(after)

        lax.fori_loop(0, 16, body, tuple(jnp.int32(0) for _ in range(8)))

    def home_slots():
        def body(slot, carry):
            target = owners[slot]
            mine = routing[target, worker, owner]
            count = jnp.int32(0)
            for i in range(16):
                count += jnp.where((routing[target, worker, i] == mine) & (i < owner), 1, 0)
            tab[HOME, slot] = 2 * worker + count
            return carry

        lax.fori_loop(0, 16, body, 0)

    stages = (stage0, stage1)

    def fetch(n, at):
        columns = pl.ds(PART * half_of_unit(n), PART)
        return pltpu.make_async_copy(
            emb.at[:, pl.ds(ROWS * chunk_of_unit(n), ROWS), columns], stages[at], stage_sem.at[at]
        )

    lane = lax.broadcasted_iota(jnp.int32, (1, TILE), 1)
    eye = lax.broadcasted_iota(jnp.int32, (TILE, TILE), 0) == lax.broadcasted_iota(jnp.int32, (TILE, TILE), 1)
    chunk_half = lax.broadcasted_iota(jnp.int32, (8, 128), 0)
    place_half = lax.broadcasted_iota(jnp.int32, (8, 128), 1) // 16
    on_place = place_half == chunk_half

    def spread(x):
        for shift in (64, 32, 16):
            x = x + pltpu.roll(x, shift, 1)
        return x

    def label_tiles():
        for block in range(16):
            row = lab[block : block + 1, :].astype(jnp.float32)
            lab_0[block] = spread(jnp.where(on_place, row, 0.0))

    steps = STEPS
    order = [step[1] for step in steps if step[0] == "go" and step[2] == 0]
    fetch(order[0], 0).start()
    fetch(order[1], 1).start()
    invert(SENT, lambda i: owners[i], lambda i: i)
    prepared = []

    def prepare(n):
        at = len(prepared)
        prepared.append(n)
        fetch(n, at % 2).wait()
        permute(SENT if kind(n) in "AB" else FIRST, stages[at % 2], sends[n], flat=True)
        if at + 2 < UNITS:
            fetch(order[at + 2], at % 2).start()

    def as_column(row):
        column = jnp.transpose(jnp.broadcast_to(row, (128, TILE)))
        return jnp.concatenate([column, column], axis=1)

    def product(i, j, half):
        a = members[half, i].reshape(TILE, PART)
        b = members[half, j].reshape(TILE, PART)
        return lax.dot_general(a, b, (((1,), (1,)), ((), ())), preferred_element_type=jnp.float32)

    def base(i):
        return sum(range(LATE + 1, i + 1))

    def gram_first(i):
        def body(j, carry):
            partial[base(i) + j] = product(i, j, 0)
            return carry

        lax.fori_loop(0, i + 1, body, 0)

    def full(i, j):
        if i >= LATE:
            return partial[base(i) + j] + product(i, j, 1)
        return product(i, j, 0) + product(i, j, 1)

    def gram_labels(i):
        n = ARRIVALS[i]
        row = jnp.zeros((1, TILE), jnp.float32)
        for slot in range(16):
            if n < 4:
                tile = lab_e[slot // 4, slot % 4]
            else:
                index = tab[PLACES, slot]
                tile = lab_e[index >> 2, index & 3]
            piece = tile[n : n + 1, :]
            row = jnp.where(lane // 16 == slot, jnp.concatenate([piece, piece], axis=1), row)
        label_rows[i] = jnp.broadcast_to(row, (8, TILE))

    def gram(i):
        row = label_rows[i][0:1]
        labels = as_column(row)
        own = full(i, i)
        scale = lax.rsqrt(jnp.sum(jnp.where(eye, own, 0.0), axis=0, keepdims=True) / WIDTH + 1e-6)
        scale_rows[i] = jnp.broadcast_to(scale, (8, TILE))
        scales = as_column(scale)
        scored = jnp.where((labels == row) & jnp.logical_not(eye), own * scales, NEG)
        best_rows[i] = jnp.broadcast_to(jnp.max(scored, axis=0, keepdims=True), (8, TILE))
        lane_best[...] = jnp.full((TILE, 128), NEG, jnp.float32)

        def body(j, carry):
            other = full(i, j)
            match = labels == label_rows[j][0:1]
            down = jnp.max(jnp.where(match, other * scales, NEG), axis=0, keepdims=True)
            best_rows[j] = jnp.maximum(best_rows[j], jnp.broadcast_to(down, (8, TILE)))
            across = jnp.where(match, other * scale_rows[j][0:1], NEG)
            lane_best[...] = jnp.maximum(lane_best[...], jnp.maximum(across[:, :128], across[:, 128:]))
            return carry

        if i > 0:
            lax.fori_loop(0, i, body, 0)
            turned = jnp.max(jnp.transpose(lane_best[...]), axis=0, keepdims=True)
            best_rows[i] = jnp.maximum(best_rows[i], jnp.broadcast_to(turned, (8, TILE)))

    greeted = []
    arrived = set()
    for step in steps:
        if step[0] == "go":
            _, n, stage = step
            if stage == 0 and n not in prepared:
                if kind(n) in "CD" and not any(kind(m) in "CD" for m in prepared):
                    ranked(KEY, lambda i: routing[i, worker, owner])
                    invert(FIRST, lambda i: tab[KEY, i], lambda i: tab[SENT, i])
                prepare(n)
            if not greeted:
                greeted.append(True)
                pl.semaphore_wait(barrier, len(O_STEPS) + len(Y_STEPS))
            go(n, stage)
        elif step[0] == "ready":
            label_tiles()
            permute(SENT, lab_0, lab_a, flat=True)
            go(LABELS, 0)
            ranked(KEY, lambda i: routing[owner, worker, i])
            invert(MID_SOURCE, lambda i: tab[KEY, i], lambda i: i)
            find(MID_TARGET, lambda i, w: routing[i, w, owner])
            find(PLACES, lambda i, w: routing[owner, w, i])
            home_slots()
            while len(prepared) < UNITS:
                prepare(order[len(prepared)])
        elif step[0] == "wait":
            _, n, stage = step
            wait(n, stage)
            if kind(n) == "A" and n % 4 == 1 and stage < 2:
                wait(LABELS, stage)
                if stage == 1:
                    middle(LABELS)
                go(LABELS, stage + 1)
        elif step[0] == "middle":
            middle(step[1])
        else:
            n = step[1]
            if not arrived:
                wait(LABELS, 2)
                for i in range(CHUNKS):
                    gram_labels(i)
            arrived.add(n)
            i = ARRIVALS.index(chunk_of_unit(n))
            if half_of_unit(n) == 1 or i >= LATE:
                assert all(2 * m + h in arrived for m in ARRIVALS[: i + 1] for h in range(half_of_unit(n) + 1)), "order"
            if half_of_unit(n) == 1:
                gram(i)
            elif i >= LATE:
                gram_first(i)

    for i, n in enumerate(ARRIVALS):
        result[n : n + 1, :] = jnp.maximum(best_rows[i][0:1] * scale_rows[i][0:1] / WIDTH, -1.0)
    back = [
        remote(result, gathered.at[worker], res_send.at[i], res_recv.at[i], (owner, worker_of(dy, dc)))
        for i, (dy, dc) in enumerate(Y_STEPS)
    ]
    for copy in back:
        copy.start()
    gathered[worker] = result[...]
    for copy in back:
        copy.wait()
    for slot in range(16):
        relayed[slot] = gathered[routing[owner, worker, slot]]
    back = [
        remote(relayed.at[owner_of(dz, dx)], home.at[owner], home_send.at[i], home_recv.at[i], (owner_of(dz, dx), worker))
        for i, (dz, dx) in enumerate(O_STEPS)
    ]
    for copy in back:
        copy.start()
    home[owner] = relayed[owner]
    for copy in back:
        copy.wait()

    chunk = lax.broadcasted_iota(jnp.int32, (8, TILE), 0)
    place = lax.broadcasted_iota(jnp.int32, (8, TILE), 1) // 16
    kept = []
    for block in range(16):
        tile = home[owners[block]]
        tile = jnp.where(place == jnp.where(chunk < 4, tab[HOME, block], owner), tile, 0.0)
        kept.append(tile[:, :128] + tile[:, 128:])
    for block in range(16):
        tile = jnp.where(on_place, spread(kept[block]), 0.0)
        out[block : block + 1, :] = jnp.sum(tile, axis=0, keepdims=True)


def shards(embeddings, row_cluster, block_owner, routing):
    vmem = pl.BlockSpec(memory_space=pltpu.VMEM)
    smem = pl.BlockSpec(memory_space=pltpu.SMEM)
    anywhere = pl.BlockSpec(memory_space=pl.ANY)
    unit = (4, 4, ROWS, PART)
    small = (4, 4, 8, 128)
    late = sum(range(LATE + 1, CHUNKS + 1))
    out, _ = pl.pallas_call(
        kernel,
        out_shape=(
            jax.ShapeDtypeStruct((16, 128), jnp.float32),
            jax.ShapeDtypeStruct((UNITS, *unit), jnp.bfloat16),
        ),
        in_specs=[smem, smem, anywhere, vmem],
        out_specs=(vmem, anywhere),
        scratch_shapes=[
            *[pltpu.VMEM(unit, jnp.bfloat16) for _ in range(UNITS)],
            *[pltpu.VMEM(unit, jnp.bfloat16) for _ in range(UNITS)],
            pltpu.VMEM((HALVES, CHUNKS, *unit), jnp.bfloat16),
            *[pltpu.VMEM((16, ROWS, PART), jnp.bfloat16) for _ in range(2)],
            pltpu.VMEM((16, 8, 128), jnp.float32),
            *[pltpu.VMEM(small, jnp.float32) for _ in range(5)],
            *[pltpu.VMEM((CHUNKS, 8, TILE), jnp.float32) for _ in range(3)],
            pltpu.VMEM((TILE, 128), jnp.float32),
            pltpu.VMEM((late, TILE, TILE), jnp.float32),
            pltpu.VMEM((8, TILE), jnp.float32),
            pltpu.VMEM((8, 8, TILE), jnp.float32),
            pltpu.VMEM((16, 8, TILE), jnp.float32),
            pltpu.VMEM((16, 8, TILE), jnp.float32),
            pltpu.SMEM((8, 16), jnp.int32),
            pltpu.SemaphoreType.DMA((UNITS + 1, 3, 7)),
            pltpu.SemaphoreType.DMA((UNITS + 1, 3, 7)),
            pltpu.SemaphoreType.DMA((UNITS + 1, 3)),
            pltpu.SemaphoreType.DMA((2,)),
            pltpu.SemaphoreType.DMA((7,)),
            pltpu.SemaphoreType.DMA((7,)),
            pltpu.SemaphoreType.DMA((15,)),
            pltpu.SemaphoreType.DMA((15,)),
        ],
        compiler_params=pltpu.CompilerParams(
            collective_id=0, has_side_effects=True, vmem_limit_bytes=62 * 2**20
        ),
        cost_estimate=pl.CostEstimate(flops=2 * 36 * 256 * 256 * 4096, bytes_accessed=64 * 2**20, transcendentals=2048),
    )(block_owner, routing, embeddings.reshape(16, 128, WIDTH), row_cluster.reshape(16, 128))
    return out.reshape(-1)


def solution(mesh):
    placed = (P(("owner", "worker"), None), P(("owner", "worker")), P(("owner", "worker")), P())
    return jax.shard_map(
        shards, mesh=mesh, in_specs=placed, out_specs=P(("owner", "worker")), check_vma=False
    )
```

time: 239 us -> 222 us (0.929)
  local copies, waits for them, and re-layouts: 8.57 us -> 1.3 us
  Pallas kernels: 226 us -> 221 us
  other arithmetic: 3.83 us -> 0 us
    pallas_call x1, Pallas kernels: 226 us -> 221 us  [shards(): pl.pallas_call(kernel, out_shape=(jax.ShapeDtypeStruct((16, 128), jnp.flo...]
    dynamic_slice x3 -> x0, local copies, waits for them, and re-layouts: 3.05 us -> none  [the longest x1 1.28 us: tables(): along_targets = routing[:, worker, owner]]
    another operation x4 -> x0, local copies, waits for them, and re-layouts: 2.45 us -> none  [the longest x1 1.26 us: tables(): jnp.stack([sent, row1, row2, row3, row4, along_sources, row6, block_owner])]
where the time goes in v2:
time: 222 us
  Pallas kernels  221 us (100%)
    pallas_call x1, Pallas kernels, shards(): pl.pallas_call(kernel, out_shape=(jax.ShapeDtypeStruct((16, 128), jnp.flo...  221 us

profile of v2, /device:TPU:1, one launch (start us, length us, event | category | flops | bytes accessed | tf_op | source)
XLA Modules:
  0.0 221.8 jit_solution(8036076748249027642)
XLA Ops:
  0.0 220.5 %shard_map.46 = (f32[16,128]{1,0:T(8,128)}, bf16[16,4,4,16,2048]{4,3,2,1,0:T(8,128)(2,1)}) custom-call(s32[16]{0:T(128)} %owners.1, s32[16,8,16]{2,1,0:T(8,128)} %routing.1, bf16[16,128,4096]{2,1,0:T(8,128)(2,1)} %bitcast.4, s32[16,128]{1,0:T(8,128)} %bitcast.5), custom_call_target="tpu_custom_call" | custom-call | flops 19327352832 | bytes 67108864 | tf_op jit(solution)/shard_map/pallas_call | solution.py:423
  220.5 1.3 copy.6

commit v3 on v2

v3 whole, which is shorter than its diff:
```python
import jax
import jax.numpy as jnp
from jax import lax
from jax.experimental import pallas as pl
from jax.experimental.pallas import tpu as pltpu
from jax.sharding import PartitionSpec as P

MESH = pl.DeviceIdType.MESH
CHUNKS = 8
PARTS = 5
UNITS = 4 * PARTS
ROWS = 16
WIDTH = 4096
WIDEST = 2048
STAGES = 3
CUTS = ((0, 2048), (2048, 2048), (0, 2048), (2048, 1280), (3328, 768))
TILE = 256
NEG = -3.0e38
FAR = -1.0e30
FLYING = 2
AXES = {"A": "zxy", "B": "xzy", "C": "yzx", "D": "yxz"}
Y_STEPS = ((1, 0), (3, 1), (2, 0), (1, 1), (3, 0), (2, 1), (0, 1))
O_STEPS = tuple((a, b) for a in range(4) for b in range(4) if (a, b) != (0, 0))
LATE = 5
LABELS = UNITS
SENT, FIRST, MID_SOURCE, MID_TARGET, PLACES, KEY, HOME = range(7)


def kind(unit):
    return "ABCD"[unit // PARTS]


def chunk_of_unit(unit):
    return 2 * (unit // PARTS) + (unit % PARTS) // 2 - (unit % PARTS) // 4


def columns_of(unit):
    return CUTS[unit % PARTS]


def plan():
    steps = []
    queue = {"z": [], "x": [], "y": []}
    flying = {"z": [], "x": [], "y": []}
    free_at = {"z": 0, "x": 0, "y": 0}

    def fill(axis, now):
        while queue[axis] and len(flying[axis]) < FLYING:
            unit, stage = queue[axis].pop(0)
            free_at[axis] = max(free_at[axis], now) + columns_of(unit)[1]
            flying[axis].append((free_at[axis], unit, stage))
            steps.append(("go", unit, stage))

    for sub in range(PARTS):
        for letter in range(3):
            queue[AXES["ABCD"[letter]][0]].append((PARTS * letter + sub, 0))
    for sub in range(PARTS):
        queue["y"].append((3 * PARTS + sub, 0))
    for _ in range(FLYING):
        for axis in "zxy":
            unit, stage = queue[axis].pop(0)
            free_at[axis] += columns_of(unit)[1]
            flying[axis].append((free_at[axis], unit, stage))
            steps.append(("go", unit, stage))
    steps.append(("ready",))
    while any(flying.values()):
        now, axis = min((flying[axis][0][0], "zxy".index(axis)) for axis in "zxy" if flying[axis])
        axis = "zxy"[axis]
        _, unit, stage = flying[axis].pop(0)
        steps.append(("wait", unit, stage))
        fill(axis, now)
        if stage == 2:
            steps.append(("arrived", unit))
            continue
        if stage == (1 if kind(unit) in "AB" else 0):
            steps.append(("middle", unit))
        following = AXES[kind(unit)][stage + 1]
        queue[following].append((unit, stage + 1))
        fill(following, now)
    return steps


STEPS = plan()
ARRIVALS = tuple(chunk_of_unit(step[1]) for step in STEPS if step[0] == "arrived" and step[1] % PARTS in (1, 4))


def kernel(owners, routing_far, emb, lab_far, out, r1, *scratch):
    sends = scratch[0:UNITS]
    mids = scratch[UNITS : 2 * UNITS]
    (
        members, stage0, stage1, stage2, lab, routing, lab_0, lab_a, lab_b, lab_c, lab_d, lab_e, label_rows, scale_rows, best_rows, lane_best, partial, rest,
        result, gathered, relayed, home, tab, send_sem, recv_sem, local_sem, stage_sem, table_sem, back_sem,
    ) = scratch[2 * UNITS :]
    owner = lax.axis_index("owner")
    worker = lax.axis_index("worker")
    mz, mx = owner // 4, owner % 4
    my, mc = worker // 2, worker % 2

    def turn(value, step, size):
        return lax.rem(value + step, size)

    def owner_of(dz, dx):
        return turn(mz, dz, 4) * 4 + turn(mx, dx, 4)

    def worker_of(dy, dc):
        return turn(my, dy, 4) * 2 + turn(mc, dc, 2)

    stages = (stage0, stage1, stage2)

    def fetch(n, at):
        first, width = columns_of(n)
        return pltpu.make_async_copy(
            emb.at[:, pl.ds(ROWS * chunk_of_unit(n), ROWS), pl.ds(first, width)],
            stages[at].at[:, :, pl.ds(0, width)],
            stage_sem.at[at],
        )

    steps = STEPS
    order = [step[1] for step in steps if step[0] == "go" and step[2] == 0]
    for at in range(STAGES):
        fetch(order[at], at).start()
    routing_copy = pltpu.make_async_copy(routing_far, routing, table_sem.at[0])
    routing_copy.start()
    lab_copy = pltpu.make_async_copy(lab_far, lab, table_sem.at[1])
    lab_copy.start()
    barrier = pltpu.get_barrier_semaphore()
    for dz, dx in O_STEPS:
        pl.semaphore_signal(barrier, inc=1, device_id=(owner_of(dz, dx), worker), device_id_type=MESH)
    for dy, dc in Y_STEPS:
        pl.semaphore_signal(barrier, inc=1, device_id=(owner, worker_of(dy, dc)), device_id_type=MESH)

    def remote(src, dst, send, recv, to):
        return pltpu.make_async_remote_copy(
            src_ref=src, dst_ref=dst, send_sem=send, recv_sem=recv, device_id=to, device_id_type=MESH
        )

    def hop(axis, src, dst, send, recv, local):
        copies = []
        if axis == "z":
            for d in (1, 3, 2):
                to = turn(mz, d, 4)
                copies.append(remote(src.at[to], dst.at[mz], send, recv, (to * 4 + mx, worker)))
            here = (src.at[mz], dst.at[mz])
        elif axis == "x":
            for d in (1, 3, 2):
                to = turn(mx, d, 4)
                copies.append(remote(src.at[:, to], dst.at[:, mx], send, recv, (mz * 4 + to, worker)))
            here = (src.at[:, mx], dst.at[:, mx])
        else:
            for dy, dc in Y_STEPS:
                to = worker_of(dy, dc)
                copies.append(
                    remote(src.at[to // 2, pl.ds(2 * lax.rem(to, 2), 2)], dst.at[my, pl.ds(2 * mc, 2)], send, recv, (owner, to))
                )
            here = (src.at[my, pl.ds(2 * mc, 2)], dst.at[my, pl.ds(2 * mc, 2)])
        copies.append(pltpu.make_async_copy(here[0], here[1], local))
        return copies

    flying = {}
    started = {"z": 0, "x": 0, "y": 0}

    def all_of(like, sem):
        pltpu.make_async_copy(like, like, sem).wait()

    def wait(n, stage):
        axis, local, place = flying.pop((n, stage))
        like = size_of(n, axis)
        all_of(like, recv_sem.at[n, stage])
        local.wait()

    def size_of(n, axis):
        blocks = 14 if axis == "y" else 12
        return lab_0.at[pl.ds(0, blocks)] if n == LABELS else stage0.at[pl.ds(0, blocks), :, pl.ds(0, columns_of(n)[1])]

    sending = {}

    def sent(place):
        if place in sending:
            n, axis = sending.pop(place)
            all_of(size_of(n, axis), send_sem.at[place])

    def permute(row, src, dst, flat=False, width=None):
        def body(slot, carry):
            index = tab[row, slot]
            if width is not None:
                dst[slot >> 2, slot & 3] = src[index, :, pl.ds(0, width)]
            elif flat:
                dst[slot >> 2, slot & 3] = src[index]
            else:
                dst[slot >> 2, slot & 3] = src[index >> 2, index & 3]
            return carry

        lax.fori_loop(0, 16, body, 0)

    def route(n):
        if n == LABELS:
            return "zxy", ((lab_a, lab_b), (lab_b, lab_c), (lab_d, lab_e))
        columns = pl.ds(*columns_of(n))
        s, r, m = sends[n], r1.at[chunk_of_unit(n), :, :, :, columns], mids[n]
        f = members.at[ARRIVALS.index(chunk_of_unit(n)), :, :, :, columns]
        return AXES[kind(n)], ((s, r), (r, m), (s, f)) if kind(n) in "AB" else ((s, m), (s, r), (r, f))

    def go(n, stage):
        axes, ends = route(n)
        axis = axes[stage]
        if n == LABELS:
            place = (3, stage)
        else:
            place = ("zxy".index(axis), started[axis] % (FLYING + 1))
            started[axis] += 1
        sent(place)
        sending[place] = (n, axis)
        copies = hop(axis, *ends[stage], send_sem.at[place], recv_sem.at[n, stage], local_sem.at[place])
        flying[n, stage] = (axis, copies[-1], place)
        for copy in copies:
            copy.start()

    def middle(n):
        for place in [place for place in sending if sending[place][0] == n]:
            sent(place)
        if n == LABELS:
            permute(MID_SOURCE, lab_c, lab_d)
        else:
            permute(MID_SOURCE if kind(n) in "AB" else MID_TARGET, mids[n], sends[n])

    def invert(row, keys, payload):
        def body(slot, carry):
            found = jnp.int32(0)
            for i in range(16):
                found += jnp.where(keys(i) == slot, payload(i), 0)
            tab[row, slot] = found & 15
            return carry

        lax.fori_loop(0, 16, body, 0)

    def ranked(row, values):
        def body(slot, carry):
            value = values(slot)
            count = jnp.int32(0)
            for i in range(16):
                count += jnp.where((values(i) == value) & (i < slot), 1, 0)
            tab[row, slot] = 2 * value + count
            return carry

        lax.fori_loop(0, 16, body, 0)

    def find(row, values):
        def body(slot, counts):
            found = jnp.int32(0)
            after = []
            for w in range(8):
                hit = values(slot, w) == worker
                found += jnp.where(hit, 2 * w + counts[w], 0)
                after.append(counts[w] + jnp.where(hit, 1, 0))
            tab[row, slot] = found & 15
            return tuple(after)

        lax.fori_loop(0, 16, body, tuple(jnp.int32(0) for _ in range(8)))

    def home_slots():
        def body(slot, carry):
            target = owners[slot]
            mine = routing[target, worker, owner]
            count = jnp.int32(0)
            for i in range(16):
                count += jnp.where((routing[target, worker, i] == mine) & (i < owner), 1, 0)
            tab[HOME, slot] = 2 * worker + count
            return carry

        lax.fori_loop(0, 16, body, 0)

    lane = lax.broadcasted_iota(jnp.int32, (1, TILE), 1)
    eye = lax.broadcasted_iota(jnp.int32, (TILE, TILE), 0) == lax.broadcasted_iota(jnp.int32, (TILE, TILE), 1)
    chunk_half = lax.broadcasted_iota(jnp.int32, (8, 128), 0)
    place_half = lax.broadcasted_iota(jnp.int32, (8, 128), 1) // 16
    on_place = place_half == chunk_half

    def spread(x):
        for shift in (64, 32, 16):
            x = x + pltpu.roll(x, shift, 1)
        return x

    def label_tiles():
        for block in range(16):
            row = lab[block : block + 1, :].astype(jnp.float32)
            lab_0[block] = spread(jnp.where(on_place, row, 0.0))

    invert(SENT, lambda i: owners[i], lambda i: i)
    prepared = []

    def prepare(n):
        at = len(prepared)
        prepared.append(n)
        fetch(n, at % STAGES).wait()
        permute(SENT if kind(n) in "AB" else FIRST, stages[at % STAGES], sends[n], width=columns_of(n)[1])
        if at + STAGES < UNITS:
            fetch(order[at + STAGES], at % STAGES).start()

    def as_column(row):
        column = jnp.transpose(jnp.broadcast_to(row, (128, TILE)))
        return jnp.concatenate([column, column], axis=1)

    def product(first, count, j, columns):
        a = members[first : first + count, :, :, :, columns].reshape(count * TILE, columns.stop - columns.start)
        b = members[j, :, :, :, columns].reshape(TILE, columns.stop - columns.start)
        return lax.dot_general(a, b, (((1,), (1,)), ((), ())), preferred_element_type=jnp.float32)

    whole = slice(0, WIDTH)
    late_count = CHUNKS - LATE

    def part(level):
        first, width = CUTS[2 + level]
        return slice(first, first + width)

    def wide(at):
        column = rest[at * TILE : (at + 1) * TILE]
        return jnp.concatenate([column, column], axis=1)

    def keep(x, labels, j):
        return jnp.where(labels == label_rows[j][0:1], x, FAR)

    def late_products(level):
        if level == 0:
            for at in range(late_count):
                rest[at * TILE : (at + 1) * TILE] = as_column(label_rows[LATE + at][0:1])[:, :128]

        def body(j, carry):
            total = product(LATE, late_count, j, part(level))
            for at in range(late_count):
                rows = slice(at * TILE, (at + 1) * TILE)
                if level == 0:
                    partial[j, rows] = keep(total[rows], wide(at), j)
                else:
                    partial[j, rows] = partial[j, rows] + total[rows]
            return carry

        lax.fori_loop(0, LATE, body, 0)
        for j in range(LATE, CHUNKS):
            total = product(j, CHUNKS - j, j, part(level))
            for i in range(j, CHUNKS):
                rows, own = slice((i - LATE) * TILE, (i - LATE + 1) * TILE), total[(i - j) * TILE : (i - j + 1) * TILE]
                if level > 0:
                    own = own + partial[j, rows]
                elif i > j:
                    own = keep(own, wide(i - LATE), j)
                partial[j, rows] = own

    def gram_labels(i):
        n = ARRIVALS[i]
        row = jnp.zeros((1, TILE), jnp.float32)
        for slot in range(16):
            if n < 4:
                tile = lab_e[slot // 4, slot % 4]
            else:
                index = tab[PLACES, slot]
                tile = lab_e[index >> 2, index & 3]
            piece = tile[n : n + 1, :]
            row = jnp.where(lane // 16 == slot, jnp.concatenate([piece, piece], axis=1), row)
        label_rows[i] = jnp.broadcast_to(row, (8, TILE))

    def own_scores(i, own):
        row = label_rows[i][0:1]
        labels = as_column(row)
        scale = lax.rsqrt(jnp.sum(jnp.where(eye, own, 0.0), axis=0, keepdims=True) / WIDTH + 1e-6)
        scale_rows[i] = jnp.broadcast_to(scale, (8, TILE))
        scales = as_column(scale)
        scored = jnp.where((labels == row) & jnp.logical_not(eye), own * scales, NEG)
        best_rows[i] = jnp.broadcast_to(jnp.max(scored, axis=0, keepdims=True), (8, TILE))
        return labels, scales

    def pair(other, scales, j):
        down = jnp.max(other * scales, axis=0, keepdims=True)
        best_rows[j] = jnp.maximum(best_rows[j], jnp.broadcast_to(down, (8, TILE)))
        across = other * scale_rows[j][0:1]
        return jnp.maximum(across[:, :128], across[:, 128:])

    def settle(i, at):
        turned = jnp.max(jnp.transpose(lane_best[at]), axis=0, keepdims=True)
        best_rows[i] = jnp.maximum(best_rows[i], jnp.broadcast_to(turned, (8, TILE)))

    def gram(i):
        labels, scales = own_scores(i, product(i, 1, i, whole))
        lane_best[0] = jnp.full((TILE, 128), NEG, jnp.float32)

        def body(j, carry):
            lane_best[0] = jnp.maximum(lane_best[0], pair(keep(product(i, 1, j, whole), labels, j), scales, j))
            return carry

        if i > 0:
            lax.fori_loop(0, i, body, 0)
            settle(i, 0)

    def late_gram():
        last = part(2)
        scales = [None] * late_count
        for at in range(late_count):
            lane_best[at] = jnp.full((TILE, 128), NEG, jnp.float32)
        for j in range(LATE, CHUNKS):
            at = j - LATE
            total = partial[j, at * TILE :] + product(j, CHUNKS - j, j, last)
            _, scales[at] = own_scores(j, total[:TILE])
            rest[at * TILE : (at + 1) * TILE] = scales[at][:, :128]
            partial[j, at * TILE :] = total
        for j in range(LATE, CHUNKS):
            for i in range(j + 1, CHUNKS):
                at = i - LATE
                lane_best[at] = jnp.maximum(lane_best[at], pair(partial[j, at * TILE : (at + 1) * TILE], scales[at], j))

        def body(j, carry):
            total = partial[j] + product(LATE, late_count, j, last)
            for at in range(late_count):
                lane_best[at] = jnp.maximum(lane_best[at], pair(total[at * TILE : (at + 1) * TILE], wide(at), j))
            return carry

        lax.fori_loop(0, LATE, body, 0)
        for at in range(late_count):
            settle(LATE + at, at)

    greeted = []
    done = []
    arrived = set()
    for step in steps:
        if step[0] == "go":
            _, n, stage = step
            if stage == 0 and n not in prepared:
                if kind(n) in "CD" and not any(kind(m) in "CD" for m in prepared):
                    routing_copy.wait()
                    ranked(KEY, lambda i: routing[i, worker, owner])
                    invert(FIRST, lambda i: tab[KEY, i], lambda i: tab[SENT, i])
                prepare(n)
            if not greeted:
                greeted.append(True)
                pl.semaphore_wait(barrier, len(O_STEPS) + len(Y_STEPS))
            go(n, stage)
        elif step[0] == "ready":
            lab_copy.wait()
            label_tiles()
            permute(SENT, lab_0, lab_a, flat=True)
            go(LABELS, 0)
            ranked(KEY, lambda i: routing[owner, worker, i])
            invert(MID_SOURCE, lambda i: tab[KEY, i], lambda i: i)
            find(MID_TARGET, lambda i, w: routing[i, w, owner])
            find(PLACES, lambda i, w: routing[owner, w, i])
            home_slots()
            while len(prepared) < UNITS:
                prepare(order[len(prepared)])
        elif step[0] == "wait":
            _, n, stage = step
            wait(n, stage)
            if n == 1 and stage < 2:
                wait(LABELS, stage)
                if stage == 1:
                    middle(LABELS)
                go(LABELS, stage + 1)
        elif step[0] == "middle":
            middle(step[1])
        else:
            n = step[1]
            if not arrived:
                wait(LABELS, 2)
                for i in range(CHUNKS):
                    gram_labels(i)
            arrived.add(n)
            i = ARRIVALS.index(chunk_of_unit(n))
            if n % PARTS in (1, 4) and i < LATE:
                assert all(m in arrived for m in range(UNITS) if chunk_of_unit(m) in ARRIVALS[: i + 1]), "order"
                gram(i)
            while len(done) < 3:
                level = len(done)
                after = {m for m in range(UNITS) if chunk_of_unit(m) in ARRIVALS[LATE:] and m % PARTS > 2 + level}
                if arrived | after != set(range(UNITS)):
                    break
                done.append(level)
                if level < 2:
                    late_products(level)
                else:
                    late_gram()
    assert len(done) == 3, "order"

    for i, n in enumerate(ARRIVALS):
        result[n : n + 1, :] = jnp.maximum(best_rows[i][0:1] * scale_rows[i][0:1] / WIDTH, -1.0)
    for dy, dc in Y_STEPS:
        remote(result, gathered.at[worker], back_sem.at[0], back_sem.at[1], (owner, worker_of(dy, dc))).start()
    gathered[worker] = result[...]
    all_of(gathered.at[pl.ds(0, 7)], back_sem.at[1])
    for slot in range(16):
        relayed[slot] = gathered[routing[owner, worker, slot]]
    for dz, dx in O_STEPS:
        to = owner_of(dz, dx)
        remote(relayed.at[to], home.at[owner], back_sem.at[2], back_sem.at[3], (to, worker)).start()
    home[owner] = relayed[owner]
    all_of(home.at[pl.ds(0, 15)], back_sem.at[3])

    chunk = lax.broadcasted_iota(jnp.int32, (8, TILE), 0)
    place = lax.broadcasted_iota(jnp.int32, (8, TILE), 1) // 16
    kept = []
    for block in range(16):
        tile = home[owners[block]]
        tile = jnp.where(place == jnp.where(chunk < 4, tab[HOME, block], owner), tile, 0.0)
        kept.append(tile[:, :128] + tile[:, 128:])
    for block in range(16):
        tile = jnp.where(on_place, spread(kept[block]), 0.0)
        out[block : block + 1, :] = jnp.sum(tile, axis=0, keepdims=True)
    all_of(gathered.at[pl.ds(0, 7)], back_sem.at[0])
    all_of(home.at[pl.ds(0, 15)], back_sem.at[2])
    for place in list(sending):
        sent(place)


def shards(embeddings, row_cluster, block_owner, routing):
    vmem = pl.BlockSpec(memory_space=pltpu.VMEM)
    smem = pl.BlockSpec(memory_space=pltpu.SMEM)
    anywhere = pl.BlockSpec(memory_space=pl.ANY)
    whole = (CHUNKS, 4, 4, ROWS, WIDTH)
    units = [pltpu.VMEM((4, 4, ROWS, columns_of(n)[1]), jnp.bfloat16) for n in range(UNITS)]
    small = (4, 4, 8, 128)
    out, _ = pl.pallas_call(
        kernel,
        out_shape=(jax.ShapeDtypeStruct((16, 128), jnp.float32), jax.ShapeDtypeStruct(whole, jnp.bfloat16)),
        in_specs=[smem, anywhere, anywhere, anywhere],
        out_specs=(vmem, anywhere),
        scratch_shapes=[
            *units,
            *units,
            pltpu.VMEM(whole, jnp.bfloat16),
            *[pltpu.VMEM((16, ROWS, WIDEST), jnp.bfloat16) for _ in range(STAGES)],
            pltpu.VMEM((16, 128), jnp.int32),
            pltpu.SMEM((16, 8, 16), jnp.int32),
            pltpu.VMEM((16, 8, 128), jnp.float32),
            *[pltpu.VMEM(small, jnp.float32) for _ in range(5)],
            *[pltpu.VMEM((CHUNKS, 8, TILE), jnp.float32) for _ in range(3)],
            pltpu.VMEM((CHUNKS - LATE, TILE, 128), jnp.float32),
            pltpu.VMEM((CHUNKS, (CHUNKS - LATE) * TILE, TILE), jnp.float32),
            pltpu.VMEM((2 * (CHUNKS - LATE) * TILE, 128), jnp.float32),
            pltpu.VMEM((8, TILE), jnp.float32),
            pltpu.VMEM((8, 8, TILE), jnp.float32),
            pltpu.VMEM((16, 8, TILE), jnp.float32),
            pltpu.VMEM((16, 8, TILE), jnp.float32),
            pltpu.SMEM((8, 16), jnp.int32),
            pltpu.SemaphoreType.DMA((4, FLYING + 1)),
            pltpu.SemaphoreType.DMA((UNITS + 1, 3)),
            pltpu.SemaphoreType.DMA((4, FLYING + 1)),
            pltpu.SemaphoreType.DMA((STAGES,)),
            pltpu.SemaphoreType.DMA((2,)),
            pltpu.SemaphoreType.DMA((4,)),
        ],
        compiler_params=pltpu.CompilerParams(
            collective_id=0, has_side_effects=True, vmem_limit_bytes=62 * 2**20
        ),
        cost_estimate=pl.CostEstimate(flops=2 * 36 * 256 * 256 * 4096, bytes_accessed=64 * 2**20, transcendentals=2048),
    )(block_owner, routing, embeddings.reshape(16, 128, WIDTH), row_cluster.reshape(16, 128))
    return out.reshape(-1)


def solution(mesh):
    placed = (P(("owner", "worker"), None), P(("owner", "worker")), P(("owner", "worker")), P())
    return jax.shard_map(
        shards, mesh=mesh, in_specs=placed, out_specs=P(("owner", "worker")), check_vma=False
    )
```

time: 222 us -> 211 us (0.950)
  Pallas kernels: 221 us -> 209 us
    pallas_call x1, Pallas kernels: 221 us -> 209 us  [shards(): pl.pallas_call(kernel, out_shape=(jax.ShapeDtypeStruct((16, 128), jnp.flo...]
where the time goes in v3:
time: 211 us; the launch traced here: 210 us
  Pallas kernels  209 us (99%)
    pallas_call x1, Pallas kernels, shards(): pl.pallas_call(kernel, out_shape=(jax.ShapeDtypeStruct((16, 128), jnp.flo...  209 us

profile of v3, /device:TPU:1, one launch (start us, length us, event | category | flops | bytes accessed | tf_op | source)
XLA Modules:
  0.0 210.4 jit_solution(14176434506430013103)
XLA Ops:
  0.0 209.1 %shard_map.46 = (f32[16,128]{1,0:T(8,128)}, bf16[8,4,4,16,4096]{4,3,2,1,0:T(8,128)(2,1)}) custom-call(s32[16]{0:T(128)} %owners.1, s32[16,8,16]{2,1,0:T(8,128)} %routing_far.1, bf16[16,128,4096]{2,1,0:T(8,128)(2,1)} %bitcast.4, s32[16,128]{1,0:T(8,128)} %bitcast.5), custom_call_target="tpu_custom_call" | custom-call | flops 19327352832 | bytes 67108864 | tf_op jit(solution)/shard_map/pallas_call | solution.py:517
  209.1 1.3 copy.6

commit v4 on v3

--- a/solution.py
+++ b/solution.py
@@ -7,19 +7,20 @@
 
 MESH = pl.DeviceIdType.MESH
 CHUNKS = 8
-PARTS = 5
+PARTS = 7
 UNITS = 4 * PARTS
 ROWS = 16
 WIDTH = 4096
 WIDEST = 2048
-STAGES = 3
-CUTS = ((0, 2048), (2048, 2048), (0, 2048), (2048, 1280), (3328, 768))
+STAGES = 4
+CUTS = ((0, 512), (512, 1536), (2048, 2048), (0, 1792), (1792, 1024), (2816, 768), (3584, 512))
+LEVELS = 4
 TILE = 256
 NEG = -3.0e38
 FAR = -1.0e30
-FLYING = 2
+FLYING = 3
 AXES = {"A": "zxy", "B": "xzy", "C": "yzx", "D": "yxz"}
-Y_STEPS = ((1, 0), (3, 1), (2, 0), (1, 1), (3, 0), (2, 1), (0, 1))
+Y_STEPS = ((2, 0), (2, 1), (1, 0), (3, 1), (1, 1), (3, 0), (0, 1))
 O_STEPS = tuple((a, b) for a in range(4) for b in range(4) if (a, b) != (0, 0))
 LATE = 5
 LABELS = UNITS
@@ -31,7 +32,7 @@
 
 
 def chunk_of_unit(unit):
-    return 2 * (unit // PARTS) + (unit % PARTS) // 2 - (unit % PARTS) // 4
+    return 2 * (unit // PARTS) + (1 if unit % PARTS >= 3 else 0)
 
 
 def columns_of(unit):
@@ -81,14 +82,14 @@
 
 
 STEPS = plan()
-ARRIVALS = tuple(chunk_of_unit(step[1]) for step in STEPS if step[0] == "arrived" and step[1] % PARTS in (1, 4))
+ARRIVALS = tuple(chunk_of_unit(step[1]) for step in STEPS if step[0] == "arrived" and step[1] % PARTS in (2, 6))
 
 
 def kernel(owners, routing_far, emb, lab_far, out, r1, *scratch):
     sends = scratch[0:UNITS]
     mids = scratch[UNITS : 2 * UNITS]
     (
-        members, stage0, stage1, stage2, lab, routing, lab_0, lab_a, lab_b, lab_c, lab_d, lab_e, label_rows, scale_rows, best_rows, lane_best, partial, rest,
+        members, stage0, stage1, stage2, stage3, lab, routing, lab_0, lab_a, lab_b, lab_c, lab_d, lab_e, label_rows, scale_rows, best_rows, lane_best, partial, rest,
         result, gathered, relayed, home, tab, send_sem, recv_sem, local_sem, stage_sem, table_sem, back_sem,
     ) = scratch[2 * UNITS :]
     owner = lax.axis_index("owner")
@@ -105,7 +106,7 @@
     def worker_of(dy, dc):
         return turn(my, dy, 4) * 2 + turn(mc, dc, 2)
 
-    stages = (stage0, stage1, stage2)
+    stages = (stage0, stage1, stage2, stage3)
 
     def fetch(n, at):
         first, width = columns_of(n)
@@ -137,12 +138,12 @@
     def hop(axis, src, dst, send, recv, local):
         copies = []
         if axis == "z":
-            for d in (1, 3, 2):
+            for d in (2, 1, 3):
                 to = turn(mz, d, 4)
                 copies.append(remote(src.at[to], dst.at[mz], send, recv, (to * 4 + mx, worker)))
             here = (src.at[mz], dst.at[mz])
         elif axis == "x":
-            for d in (1, 3, 2):
+            for d in (2, 1, 3):
                 to = turn(mx, d, 4)
                 copies.append(remote(src.at[:, to], dst.at[:, mx], send, recv, (mz * 4 + to, worker)))
             here = (src.at[:, mx], dst.at[:, mx])
@@ -309,7 +310,7 @@
     late_count = CHUNKS - LATE
 
     def part(level):
-        first, width = CUTS[2 + level]
+        first, width = CUTS[3 + level]
         return slice(first, first + width)
 
     def wide(at):
@@ -391,7 +392,7 @@
             settle(i, 0)
 
     def late_gram():
-        last = part(2)
+        last = part(LEVELS - 1)
         scales = [None] * late_count
         for at in range(late_count):
             lane_best[at] = jnp.full((TILE, 128), NEG, jnp.float32)
@@ -462,23 +463,23 @@
                     gram_labels(i)
             arrived.add(n)
             i = ARRIVALS.index(chunk_of_unit(n))
-            if n % PARTS in (1, 4) and i < LATE:
+            if n % PARTS in (2, 6) and i < LATE:
                 assert all(m in arrived for m in range(UNITS) if chunk_of_unit(m) in ARRIVALS[: i + 1]), "order"
                 gram(i)
-            while len(done) < 3:
+            while len(done) < LEVELS:
                 level = len(done)
-                after = {m for m in range(UNITS) if chunk_of_unit(m) in ARRIVALS[LATE:] and m % PARTS > 2 + level}
+                after = {m for m in range(UNITS) if chunk_of_unit(m) in ARRIVALS[LATE:] and m % PARTS > 3 + level}
                 if arrived | after != set(range(UNITS)):
                     break
                 done.append(level)
-                if level < 2:
+                if level < LEVELS - 1:
                     late_products(level)
                 else:
                     late_gram()
-    assert len(done) == 3, "order"
+    assert len(done) == LEVELS, "order"
 
     for i, n in enumerate(ARRIVALS):
-        result[n : n + 1, :] = jnp.maximum(best_rows[i][0:1] * scale_rows[i][0:1] / WIDTH, -1.0)
+        result[n : n + 1, :] = best_rows[i][0:1] * scale_rows[i][0:1] / WIDTH
     for dy, dc in Y_STEPS:
         remote(result, gathered.at[worker], back_sem.at[0], back_sem.at[1], (owner, worker_of(dy, dc))).start()
     gathered[worker] = result[...]
@@ -498,9 +499,8 @@
         tile = home[owners[block]]
         tile = jnp.where(place == jnp.where(chunk < 4, tab[HOME, block], owner), tile, 0.0)
         kept.append(tile[:, :128] + tile[:, 128:])
-    for block in range(16):
-        tile = jnp.where(on_place, spread(kept[block]), 0.0)
-        out[block : block + 1, :] = jnp.sum(tile, axis=0, keepdims=True)
+    kept = spread(jnp.concatenate(kept, axis=0)).reshape(16, 8, 128)
+    out[...] = jnp.sum(jnp.where(on_place, kept, 0.0), axis=1)
     all_of(gathered.at[pl.ds(0, 7)], back_sem.at[0])
     all_of(home.at[pl.ds(0, 15)], back_sem.at[2])
     for place in list(sending):
@@ -549,7 +549,7 @@
         ),
         cost_estimate=pl.CostEstimate(flops=2 * 36 * 256 * 256 * 4096, bytes_accessed=64 * 2**20, transcendentals=2048),
     )(block_owner, routing, embeddings.reshape(16, 128, WIDTH), row_cluster.reshape(16, 128))
-    return out.reshape(-1)
+    return jnp.maximum(out.reshape(-1), -1.0)
 
 
 def solution(mesh):

time: 211 us -> 210 us (level)
  no operation moved by 1% of the time
where the time goes in v4:
time: 210 us
  Pallas kernels  209 us (100%)
    pallas_call x1, Pallas kernels, shards(): pl.pallas_call(kernel, out_shape=(jax.ShapeDtypeStruct((16, 128), jnp.flo...  209 us

profile of v4, /device:TPU:1, one launch (start us, length us, event | category | flops | bytes accessed | tf_op | source)
XLA Modules:
  0.0 209.9 jit_solution(13366776501391364656)
XLA Ops:
  0.0 208.6 %shard_map.46 = (f32[16,128]{1,0:T(8,128)}, bf16[8,4,4,16,4096]{4,3,2,1,0:T(8,128)(2,1)}) custom-call(s32[16]{0:T(128)} %owners.1, s32[16,8,16]{2,1,0:T(8,128)} %routing_far.1, bf16[16,128,4096]{2,1,0:T(8,128)(2,1)} %bitcast.4, s32[16,128]{1,0:T(8,128)} %bitcast.5), custom_call_target="tpu_custom_call" | custom-call | flops 19327352832 | bytes 67108864 | tf_op jit(solution)/shard_map/pallas_call | solution.py:517
  208.6 1.3 maximum_bitcast_fusion

commit v5 on v4

--- a/solution.py
+++ b/solution.py
@@ -21,7 +21,10 @@
 FLYING = 3
 AXES = {"A": "zxy", "B": "xzy", "C": "yzx", "D": "yxz"}
 Y_STEPS = ((2, 0), (2, 1), (1, 0), (3, 1), (1, 1), (3, 0), (0, 1))
-O_STEPS = tuple((a, b) for a in range(4) for b in range(4) if (a, b) != (0, 0))
+HOPS = (0, 1, 2, 1)
+O_STEPS = tuple(
+    sorted(((a, b) for a in range(4) for b in range(4) if (a, b) != (0, 0)), key=lambda step: -HOPS[step[0]] - HOPS[step[1]])
+)
 LATE = 5
 LABELS = UNITS
 SENT, FIRST, MID_SOURCE, MID_TARGET, PLACES, KEY, HOME = range(7)

time: 210 us -> 210 us (level)
  no operation moved by 1% of the time
where the time goes in v5:
time: 210 us
  Pallas kernels  208 us (99%)
    pallas_call x1, Pallas kernels, shards(): pl.pallas_call(kernel, out_shape=(jax.ShapeDtypeStruct((16, 128), jnp.flo...  208 us

profile of v5, /device:TPU:1, one launch (start us, length us, event | category | flops | bytes accessed | tf_op | source)
XLA Modules:
  0.0 209.5 jit_solution(6190634469490067719)
XLA Ops:
  0.0 208.2 %shard_map.46 = (f32[16,128]{1,0:T(8,128)}, bf16[8,4,4,16,4096]{4,3,2,1,0:T(8,128)(2,1)}) custom-call(s32[16]{0:T(128)} %owners.1, s32[16,8,16]{2,1,0:T(8,128)} %routing_far.1, bf16[16,128,4096]{2,1,0:T(8,128)(2,1)} %bitcast.4, s32[16,128]{1,0:T(8,128)} %bitcast.5), custom_call_target="tpu_custom_call" | custom-call | flops 19327352832 | bytes 67108864 | tf_op jit(solution)/shard_map/pallas_call | solution.py:520
  208.2 1.3 maximum_bitcast_fusion
